TPU v7x, 32 devices: a whole 2x2x4 slice. The times are simulated.
32 devices in a mesh: layer: 2 (over y), tensor: 8 (over z, x), dp: 2 (over core).
Axes of the slice: x: 2, y: 2, z: 4, core: 2. Of those that a mesh axis runs over, the one named last changes fastest.
Arguments:
- resid_in: bfloat16 [2, 512, 4096], P('layer', 'dp', 'tensor'), may hold values from -6 to 6
- w_enc: bfloat16 [2, 4096, 4096], P('layer', 'dp', 'tensor'), may hold values from -0.09375 to 0.09375
- threshold: float32 [2, 4096], P('layer', 'tensor'), may hold values from 0.05 to 1
- block_mask: int32 [2, 4, 32], P('layer', 'dp', 'tensor'), may hold values 0 or 1
- w_dec: bfloat16 [2, 4096, 4096], P('layer', 'tensor', 'dp'), may hold values from -0.125 to 0.125
- w_cross: bfloat16 [4096, 4096], P('tensor', 'dp'), may hold values from -0.125 to 0.125
Outputs:
- recon: bfloat16 [2, 512, 4096], P('layer', 'dp', 'tensor')
All inputs are finite; a program needn't handle non-finite values. No bound on the sum of `block_mask` on one device may be relied on, other than what follows from the above.
Results may differ from a plain program's by a relative error of at most 0.0049.
Values may be sent and summed in bfloat16 or wider, within the bound.
A program may use at most 64 MiB of HBM per device.

v0:
```python
import jax
import jax.numpy as jnp
from jax import lax
from jax.sharding import PartitionSpec as P

TILE = 128
BLOCK = 128


def passed_along(value, axis, steps):
    count = lax.axis_size(axis)
    leading, last = (max(0, -steps), min(count, count - steps))
    return lax.ppermute(value, axis, [(source, source + steps) for source in range(leading, last)])


def gate_codes(preact, thresh, activity):
    tile_count, block_count = activity.shape
    shaped = preact.reshape(tile_count, TILE, block_count, BLOCK)
    limits = thresh.reshape(1, 1, block_count, BLOCK)
    gating = activity.astype(preact.dtype)[:, None, :, None]
    active = jnp.maximum(shaped - limits, 0.0) * gating
    return active.reshape(preact.shape).astype(jnp.bfloat16)


def shards(resid_in, w_enc, threshold, block_mask, w_dec, w_cross):
    features = lax.all_gather(resid_in[0], "tensor", axis=1, tiled=True)
    preact = jnp.dot(
        features,
        lax.all_gather(w_enc[0], "dp", axis=0, tiled=True),
        preferred_element_type=jnp.float32,
    )
    latent_codes = gate_codes(preact, threshold[0], block_mask[0])
    arrived = passed_along(latent_codes, "layer", 1)
    parts = lax.all_gather((w_dec[0], w_cross), "dp", axis=1, tiled=True)
    partial_value = jnp.dot(latent_codes, parts[0], preferred_element_type=jnp.float32) + jnp.dot(
        arrived, parts[1], preferred_element_type=jnp.float32
    )
    summed = lax.psum_scatter(partial_value, "tensor", scatter_dimension=1, tiled=True)
    return summed.astype(jnp.bfloat16)[None]


def solution(mesh):
    return jax.shard_map(
        shards,
        mesh=mesh,
        in_specs=(
            P("layer", "dp", "tensor"),
            P("layer", "dp", "tensor"),
            P("layer", "tensor"),
            P("layer", "dp", "tensor"),
            P("layer", "tensor", "dp"),
            P("tensor", "dp"),
        ),
        out_specs=P("layer", "dp", "tensor"),
        check_vma=False,
    )
```

profile of v0, /device:TPU:4, one launch (start us, length us, event | category | flops | bytes accessed | tf_op | source)
XLA Modules:
  0.0 212.5 jit_solution(10371970880793652734)
XLA Ops:
  6.5 0.0 copy-start
  6.5 0.0 copy-start.1
  6.5 0.0 all-gather.10.cloned.1.call-start
  6.5 0.7 all-gather.10.cloned.1.call-update
  7.3 0.0 all-gather.12.cloned.1.call-start
  7.3 0.7 all-gather.12.cloned.1.call-update
  8.0 0.0 all-gather.14.cloned.1.call-start
  8.1 0.7 all-gather.14.cloned.1.call-update
  8.7 0.0 all-gather.8.cloned.1.call-start
  8.8 0.5 all-gather.8.cloned.1.call-update
  9.3 0.0 reduce-scatter.2.cloned.1.call-start
  9.4 0.0 copy-done
  9.4 52.3 %all-gather.10.cloned.1.call-done = bf16[1,256,4096]{2,1,0:T(8,128)(2,1)} async-done(((bf16[1,256,512]{2,1,0:T(8,128)(2,1)}), bf16[1,256,4096]{2,1,0:T(8,128)(2,1)}) %all-gather.10.cloned.1.call-update) | async-done | bytes 2097168 | tf_op jit(solution)/shard_map/all_gather | solution.py:26
  61.7 13.7 %all-gather.12.cloned.1.call-done = bf16[1,4096,512]{2,1,0:T(8,128)(2,1)} async-done(((bf16[1,2048,512]{2,1,0:T(8,128)(2,1)}), bf16[1,4096,512]{2,1,0:T(8,128)(2,1)}) %all-gather.12.cloned.1.call-update) | async-done | bytes 4194320 | tf_op jit(solution)/shard_map/all_gather | solution.py:29
  75.4 0.1 mul.11
  75.5 0.0 copy-done.1
  75.6 4.1 %fusion.20 = bf16[256,512]{1,0:T(8,128)(2,1)S(1)} fusion(bf16[1,4096,512]{2,1,0:T(8,128)(2,1)} %all-gather.12.cloned.1.call-done, bf16[1,256,4096]{2,1,0:T(8,128)(2,1)} %all-gather.10.cloned.1.call-done, f32[32,8,4,128]{3,2,1,0:T(4,128)S(1)} %bitcast.37, f32[512]{0:T(512)S(1)} %bitcast.38), kind=kOutput, calls=%fused_computation.9 | convolution fusion | flops 1074266112 | bytes 7079936 | tf_op jit(solution)/shard_map/dot_general | solution.py:27
  79.6 1.3 collective-permute-start
  80.9 10.9 %all-gather.14.cloned.1.call-done = bf16[1,512,4096]{2,1,0:T(8,128)(2,1)} async-done(((bf16[1,512,2048]{2,1,0:T(8,128)(2,1)}), bf16[1,512,4096]{2,1,0:T(8,128)(2,1)}) %all-gather.14.cloned.1.call-update) | async-done | bytes 4194320 | tf_op jit(solution)/shard_map/all_gather | solution.py:34
  91.8 5.4 %fusion = f32[256,4096]{1,0:T(8,128)} fusion(bf16[256,512]{1,0:T(8,128)(2,1)S(1)} %fusion.20, bf16[1,512,4096]{2,1,0:T(8,128)(2,1)} %all-gather.14.cloned.1.call-done), kind=kOutput, calls=%fused_computation.1 | convolution fusion | flops 1073741824 | bytes 8650752 | tf_op jit(solution)/shard_map/dot_general | solution.py:35
  97.2 10.9 %all-gather.8.cloned.1.call-done = bf16[512,4096]{1,0:T(8,128)(2,1)} async-done(((bf16[512,2048]{1,0:T(8,128)(2,1)}), bf16[512,4096]{1,0:T(8,128)(2,1)}) %all-gather.8.cloned.1.call-update) | async-done | bytes 4194320 | tf_op jit(solution)/shard_map/all_gather | solution.py:34
  108.1 0.0 collective-permute-done
  108.1 6.7 %convolution_add_fusion = f32[256,4096]{1,0:T(8,128)} fusion(f32[256,4096]{1,0:T(8,128)} %fusion, bf16[256,512]{1,0:T(8,128)(2,1)S(1)} %collective-permute-done, bf16[512,4096]{1,0:T(8,128)(2,1)} %all-gather.8.cloned.1.call-done), kind=kOutput, calls=%fused_computation | convolution fusion | flops 1074790400 | bytes 12845056 | tf_op jit(solution)/shard_map/dot_general | solution.py:35
  114.8 0.0 reduce-scatter.2.cloned.1.call-update
  114.8 89.4 %reduce-scatter.2.cloned.1.call-done = f32[256,512]{1,0:T(8,128)} async-done(((f32[256,4096]{1,0:T(8,128)}), f32[256,512]{1,0:T(8,128)}) %reduce-scatter.2.cloned.1.call-update) | async-done | bytes 524304 | tf_op jit(solution)/shard_map/reduce_scatter | solution.py:38
  204.2 1.8 convert_bitcast_fusion
  (1 shorter events, 0.0 us)
Async XLA Ops:
  6.5 2.8 %copy-start = (s32[1,2,4]{2,1,0:T(2,128)S(1)}, s32[1,2,4]{2,1,0:T(2,128)}, u32[]{:S(2)}) copy-start(s32[1,2,4]{2,1,0:T(2,128)} %param.9) | copy-start | bytes 100
  6.5 69.0 %copy-start.1 = (f32[1,512]{1,0:T(1,128)S(1)}, f32[1,512]{1,0:T(1,128)}, u32[]{:S(2)}) copy-start(f32[1,512]{1,0:T(1,128)} %param.8) | copy-start | bytes 6148
  6.5 55.2 %all-gather.10.cloned.1.call-start = ((), (), s32[]{:S(2)}) async-start(), calls=%async_computation.3 | async-start | bytes 2359296 | tf_op jit(solution)/shard_map/all_gather | solution.py:26
  7.3 68.2 %all-gather.12.cloned.1.call-start = ((), (), s32[]{:S(2)}) async-start(), calls=%async_computation.4 | async-start | bytes 6291456 | tf_op jit(solution)/shard_map/all_gather | solution.py:29
  8.0 83.8 %all-gather.14.cloned.1.call-start = ((), (), s32[]{:S(2)}) async-start(), calls=%async_computation.5 | async-start | bytes 6291456 | tf_op jit(solution)/shard_map/all_gather | solution.py:34
  8.7 99.4 %all-gather.8.cloned.1.call-start = ((), (), s32[]{:S(2)}) async-start(), calls=%async_computation.1 | async-start | bytes 6291456 | tf_op jit(solution)/shard_map/all_gather | solution.py:34
  9.3 194.9 %reduce-scatter.2.cloned.1.call-start = ((), (), s32[]{:S(2)}) async-start(), calls=%async_computation.2 | async-start | bytes 4718592 | tf_op jit(solution)/shard_map/reduce_scatter | solution.py:38
  79.6 28.5 %collective-permute-start = (bf16[256,512]{1,0:T(8,128)(2,1)S(1)}, bf16[256,512]{1,0:T(8,128)(2,1)S(1)}, u32[]{:S(2)}, u32[]{:S(2)}) collective-permute-start(bf16[256,512]{1,0:T(8,128)(2,1)S(1)} %fusion.20), channel_id=1, source_target_pairs={{0,16},{1,17},{2,18},{3,19},{4,20},{5,21},{6,22},{7,23},{8,24},{9,... | collective-permute-start | bytes 786440 | tf_op jit(solution)/shard_map/ppermute | solution.py:13
Sparse Core Ops, SparseCore 0:
  9.4 52.2 all-gather.9
  63.3 12.1 all-gather.11
  77.0 14.8 all-gather.13
  93.2 14.8 all-gather.7
  115.0 89.1 reduce-scatter.1
where the time goes:
time: 214 us; the launch traced here: 212 us
  waiting for transfers between devices  180 us (84%)
  matrix products  16.2 us (8%)
  between operations  13.2 us (6%)
    reduce_scatter x1, waiting for transfers between devices, shards(): lax.psum_scatter(partial_value, 'tensor', scatter_dimension=1, tiled=True)  89.4 us
    all_gather x1, waiting for transfers between devices, shards(): features = lax.all_gather(resid_in[0], 'tensor', axis=1, tiled=True)  52.3 us
    all_gather x2, waiting for transfers between devices, shards(): parts = lax.all_gather((w_dec[0], w_cross), 'dp', axis=1, tiled=True)  21.8 us
    all_gather x1, waiting for transfers between devices, shards(): lax.all_gather(w_enc[0], 'dp', axis=0, tiled=True)  13.7 us
    dot_general x1, matrix products, shards(): jnp.dot(arrived, parts[1], preferred_element_type=jnp.float32)  6.7 us
    dot_general x1, matrix products, shards(): jnp.dot(latent_codes, parts[0], preferred_element_type=jnp.float32)  5.41 us
  transfers between devices with their start and end apart: 6, of which 5 were waited for; matrix products, arithmetic and copies ran while one was open for 5% of the time, Pallas kernels for 0%

commit v1 on v0

v1 whole, which is shorter than its diff:
```python
import functools

import jax
import jax.numpy as jnp
from jax import lax
from jax.experimental import pallas as pl
from jax.experimental.pallas import tpu as pltpu
from jax.sharding import PartitionSpec as P

TILE = 128
BLOCK = 128
CHUNKS = 2
GATHER_LAG = 0
SUM_LAG = 0


def grid_of(count):
    inner = 1
    while (inner * 2) ** 2 <= count:
        inner *= 2
    return count // inner, inner


def far_first(outer):
    return [sorted(range(outer), key=lambda to: (-abs(to - at), -to if at < outer / 2 else to)) for at in range(outer)]


def kernel(
    sizes, resid, thresh, mask, w_enc, w_dec, w_cross, out,
    feat, enc_buf, dec_buf, cross_buf, codes, early, held, own, x_out, x_in, z_out, up_in, down_in,
    local_sem, w_send, w_recv, g_recv, g_zsend, g_xsend, c_send, c_recv, x_send, x_recv, z_send, up_recv, down_recv,
):
    outer, inner, dp_count = sizes
    count = outer * inner
    per_slab = count // dp_count
    part_rows, part_cols = feat.shape[2:]
    layer = lax.axis_index("layer")
    me = lax.axis_index("tensor")
    dp = lax.axis_index("dp")
    z, x = me // inner, me % inner

    def to_tensor(index):
        return {"tensor": index}

    def x_peer(step):
        return lax.rem(x + step, inner)

    def dp_peer(step):
        return {"dp": lax.rem(dp + step, dp_count)}

    other_layer = {"layer": 1 - layer}
    above, below = me + inner, me - inner
    has_above, has_below = z < outer - 1, z > 0

    weights = ((w_enc, enc_buf), (w_dec, dec_buf), (w_cross, cross_buf))

    def local_copy(which):
        source, target = weights[which]
        return pltpu.make_async_copy(source, target.at[dp], local_sem.at[which])

    def weight_copy(which, step):
        source, target = weights[which]
        return pltpu.make_async_remote_copy(
            source, target.at[dp], w_send.at[which, step - 1], w_recv.at[which, step - 1],
            device_id=dp_peer(step), device_id_type=pl.DeviceIdType.MESH,
        )

    def weight_arrival(which, step):
        source, target = weights[which]
        index = lax.rem(dp + dp_count - step, dp_count)
        return pltpu.make_async_remote_copy(
            source, target.at[index], w_send.at[which, step - 1], w_recv.at[which, step - 1],
            device_id=dp_peer(step), device_id_type=pl.DeviceIdType.MESH,
        )

    def when_used(which, act):
        if which == 2:
            pl.when(layer == 1)(act)
        else:
            act()

    for which in range(3):
        when_used(which, lambda which=which: local_copy(which).start())

    barrier = pltpu.get_barrier_semaphore()

    def greet(where):
        pl.semaphore_signal(barrier, inc=1, device_id=where, device_id_type=pl.DeviceIdType.MESH)

    for step in range(1, inner):
        greet(to_tensor(z * inner + x_peer(step)))
    for step in range(1, dp_count):
        greet(dp_peer(step))
    greet(other_layer)
    pl.when(has_above)(lambda: greet(to_tensor(above)))
    pl.when(has_below)(lambda: greet(to_tensor(below)))
    ends = (z + outer - 1) // outer + (2 * outer - 2 - z) // outer
    pl.semaphore_wait(barrier, inner - 1 + dp_count - 1 + 1 + ends)

    def rows_of(chunk):
        return pl.ds(chunk * part_rows, part_rows)

    def gather_copy(chunk, line, send_sem, where, is_own):
        index = line * inner + x
        return pltpu.make_async_remote_copy(
            resid.at[0, rows_of(chunk)] if is_own else feat.at[chunk, index], feat.at[chunk, index],
            send_sem, g_recv.at[chunk, index], device_id=to_tensor(where), device_id_type=pl.DeviceIdType.MESH,
        )

    def gather_arrival(chunk, index):
        slot = feat.at[chunk, index]
        return pltpu.make_async_remote_copy(
            slot, slot, g_zsend.at[chunk, 0, 0], g_recv.at[chunk, index],
            device_id=other_layer, device_id_type=pl.DeviceIdType.MESH,
        )

    def pass_on(chunk, distance, finish):
        is_own = distance == 0

        def act(copy):
            if finish:
                copy.wait_send()
            else:
                copy.start()

        def to_inner(line):
            for step in range(1, inner):
                act(gather_copy(chunk, line, g_xsend.at[chunk, line, step - 1], z * inner + x_peer(step), is_own))

        def upward(line):
            act(gather_copy(chunk, line, g_zsend.at[chunk, line, 0], above, is_own))

        def downward(line):
            act(gather_copy(chunk, line, g_zsend.at[chunk, line, 1], below, is_own))

        if is_own:
            pl.when(has_above)(lambda: upward(z))
            pl.when(has_below)(lambda: downward(z))
            to_inner(z)
            return

        @pl.when(z >= distance)
        def _():
            line = z - distance
            if not finish:
                gather_arrival(chunk, line * inner + x).wait_recv()
            pl.when(has_above)(lambda: upward(line))
            to_inner(line)

        @pl.when(z < outer - distance)
        def _():
            line = z + distance
            if not finish:
                gather_arrival(chunk, line * inner + x).wait_recv()
            pl.when(has_below)(lambda: downward(line))
            to_inner(line)

    steps = sorted(((c, s) for c in range(CHUNKS) for s in range(outer)), key=lambda cs: (cs[1] + GATHER_LAG * cs[0], cs[0]))
    opening = [cs for cs in steps if cs[1] == 0]
    for chunk, distance in opening:
        pass_on(chunk, distance, False)
    for which in range(3):
        for step in range(1, dp_count):
            when_used(which, lambda which=which, step=step: weight_copy(which, step).start())
    for chunk in range(CHUNKS):
        feat[chunk, me] = resid[0, chunk * part_rows:(chunk + 1) * part_rows, :]
    for chunk, distance in steps:
        if distance:
            pass_on(chunk, distance, False)

    def weights_ready(which):
        local_copy(which).wait()
        for step in range(1, dp_count):
            weight_arrival(which, step).wait_recv()

    def codes_copy(chunk):
        return pltpu.make_async_remote_copy(
            codes.at[chunk], early.at[chunk], c_send.at[chunk], c_recv.at[chunk],
            device_id=other_layer, device_id_type=pl.DeviceIdType.MESH,
        )

    def encode(chunk):
        for line in range(outer):
            for step in range(1, inner):
                gather_arrival(chunk, line * inner + x_peer(step)).wait_recv()
        total = None
        for index in range(count):
            at = (index % per_slab) * part_cols
            term = jnp.dot(
                feat[chunk, index], enc_buf[index // per_slab, at:at + part_cols, :], preferred_element_type=jnp.float32
            )
            total = term if total is None else total + term
        active = jnp.maximum(total - thresh[...], 0.0)
        tile = chunk * part_rows // TILE
        for block in range(active.shape[1] // BLOCK):
            gate = mask[0, tile, block].astype(jnp.float32)
            at = block * BLOCK
            codes[chunk, :, at:at + BLOCK] = (active[:, at:at + BLOCK] * gate).astype(jnp.bfloat16)
        pl.when(layer == 0)(lambda: codes_copy(chunk).start())

    order = far_first(outer)

    def nth(place):
        value = order[0][place]
        for at in range(1, outer):
            value = jnp.where(z == at, order[at][place], value)
        return value

    def share(chunk, index, target):
        slab = index // per_slab
        columns = pl.ds(pl.multiple_of((index % per_slab) * part_cols, part_cols), part_cols)
        target[...] = jnp.dot(codes[chunk], dec_buf[slab, :, columns], preferred_element_type=jnp.float32)

        @pl.when(layer == 1)
        def _():
            target[...] += jnp.dot(early[chunk], cross_buf[slab, :, columns], preferred_element_type=jnp.float32)

    def x_copy(chunk, step, line):
        return pltpu.make_async_remote_copy(
            x_out.at[chunk, step - 1, line], x_in.at[chunk, step - 1, line],
            x_send.at[chunk, step - 1, line], x_recv.at[chunk, step - 1, line],
            device_id=to_tensor(z * inner + x_peer(step)), device_id_type=pl.DeviceIdType.MESH,
        )

    def decode(chunk):
        pl.when(layer == 1)(lambda: codes_copy(chunk).wait_recv())
        for place in range(outer):
            line = nth(place)
            for step in range(1, inner):
                share(chunk, line * inner + x_peer(step), held)
                x_out[chunk, step - 1, line] = held[...].astype(jnp.bfloat16)
                x_copy(chunk, step, line).start()
        for place in range(outer):
            line = nth(place)
            share(chunk, line * inner + x, own.at[chunk, line])

    def up_copy(chunk, line):
        return pltpu.make_async_remote_copy(
            z_out.at[chunk, line], up_in.at[chunk, line], z_send.at[chunk, line], up_recv.at[chunk, line],
            device_id=to_tensor(above), device_id_type=pl.DeviceIdType.MESH,
        )

    def down_copy(chunk, line):
        return pltpu.make_async_remote_copy(
            z_out.at[chunk, line], down_in.at[chunk, line], z_send.at[chunk, line], down_recv.at[chunk, line],
            device_id=to_tensor(below), device_id_type=pl.DeviceIdType.MESH,
        )

    def add_up(chunk, place):
        line = nth(place)
        total = own.at[chunk, line]
        for step in range(1, inner):
            x_copy(chunk, step, line).wait_recv()
            total[...] += x_in[chunk, step - 1, line].astype(jnp.float32)

        def from_below():
            up_copy(chunk, line).wait_recv()
            total[...] += up_in[chunk, line].astype(jnp.float32)

        def from_above():
            down_copy(chunk, line).wait_recv()
            total[...] += down_in[chunk, line].astype(jnp.float32)

        if place == outer - 1:
            pl.when(has_below)(from_below)
            pl.when(has_above)(from_above)
            out[0, chunk * part_rows:(chunk + 1) * part_rows, :] = total[...].astype(jnp.bfloat16)
            return

        @pl.when(line > z)
        def _():
            pl.when(has_below)(from_below)
            z_out[chunk, line] = total[...].astype(jnp.bfloat16)
            up_copy(chunk, line).start()

        @pl.when(line < z)
        def _():
            pl.when(has_above)(from_above)
            z_out[chunk, line] = total[...].astype(jnp.bfloat16)
            down_copy(chunk, line).start()

    weights_ready(0)
    for chunk in range(CHUNKS):
        encode(chunk)
    weights_ready(1)
    pl.when(layer == 1)(lambda: weights_ready(2))
    for chunk in range(CHUNKS):
        decode(chunk)
    sums = sorted(((c, k) for c in range(CHUNKS) for k in range(outer)), key=lambda ck: (ck[1] + SUM_LAG * ck[0], ck[0]))
    for chunk, place in sums:
        add_up(chunk, place)

    for chunk, distance in steps:
        pass_on(chunk, distance, True)
    for which in range(3):
        for step in range(1, dp_count):
            when_used(which, lambda which=which, step=step: weight_copy(which, step).wait_send())
    for chunk in range(CHUNKS):
        pl.when(layer == 0)(lambda chunk=chunk: codes_copy(chunk).wait_send())
        for line in range(outer):
            for step in range(1, inner):
                x_copy(chunk, step, line).wait_send()
            pl.when(line > z)(lambda chunk=chunk, line=line: up_copy(chunk, line).wait_send())
            pl.when(line < z)(lambda chunk=chunk, line=line: down_copy(chunk, line).wait_send())


def shards(mesh_shape, resid_in, w_enc, threshold, block_mask, w_dec, w_cross):
    count, dp_count = mesh_shape["tensor"], mesh_shape["dp"]
    outer, inner = grid_of(count)
    _, rows, cols = resid_in.shape
    part = rows // CHUNKS
    latents = w_enc.shape[2]
    deep, wide = w_enc.shape[1], w_dec.shape[2]
    bf16, f32 = jnp.bfloat16, jnp.float32
    dma = pltpu.SemaphoreType.DMA
    vmem = pl.BlockSpec(memory_space=pltpu.VMEM)
    anywhere = pl.BlockSpec(memory_space=pl.ANY)
    return pl.pallas_call(
        functools.partial(kernel, (outer, inner, dp_count)),
        out_shape=jax.ShapeDtypeStruct((1, rows, cols), bf16),
        in_specs=[vmem, vmem, pl.BlockSpec(memory_space=pltpu.SMEM), anywhere, anywhere, anywhere],
        out_specs=vmem,
        scratch_shapes=[
            pltpu.VMEM((CHUNKS, count, part, cols), bf16),
            pltpu.VMEM((dp_count, deep, latents), bf16),
            pltpu.VMEM((dp_count, latents, wide), bf16),
            pltpu.VMEM((dp_count, latents, wide), bf16),
            pltpu.VMEM((CHUNKS, part, latents), bf16),
            pltpu.VMEM((CHUNKS, part, latents), bf16),
            pltpu.VMEM((part, cols), f32),
            pltpu.VMEM((CHUNKS, outer, part, cols), f32),
            pltpu.VMEM((CHUNKS, inner - 1, outer, part, cols), bf16),
            pltpu.VMEM((CHUNKS, inner - 1, outer, part, cols), bf16),
            pltpu.VMEM((CHUNKS, outer, part, cols), bf16),
            pltpu.VMEM((CHUNKS, outer, part, cols), bf16),
            pltpu.VMEM((CHUNKS, outer, part, cols), bf16),
            dma((3,)),
            dma((3, dp_count - 1)),
            dma((3, dp_count - 1)),
            dma((CHUNKS, count)),
            dma((CHUNKS, outer, 2)),
            dma((CHUNKS, outer, inner - 1)),
            dma((CHUNKS,)),
            dma((CHUNKS,)),
            dma((CHUNKS, inner - 1, outer)),
            dma((CHUNKS, inner - 1, outer)),
            dma((CHUNKS, outer)),
            dma((CHUNKS, outer)),
            dma((CHUNKS, outer)),
        ],
        compiler_params=pltpu.CompilerParams(
            collective_id=0, has_side_effects=True, vmem_limit_bytes=48 * 1024 * 1024
        ),
        cost_estimate=pl.CostEstimate(
            flops=6 * rows * latents * cols * count, bytes_accessed=6 * deep * latents * dp_count, transcendentals=0
        ),
    )(resid_in, threshold, block_mask, w_enc[0], w_dec[0], w_cross)


def solution(mesh):
    return jax.shard_map(
        functools.partial(shards, dict(mesh.shape)),
        mesh=mesh,
        in_specs=(
            P("layer", "dp", "tensor"),
            P("layer", "dp", "tensor"),
            P("layer", "tensor"),
            P("layer", "dp", "tensor"),
            P("layer", "tensor", "dp"),
            P("tensor", "dp"),
        ),
        out_specs=P("layer", "dp", "tensor"),
        check_vma=False,
    )
```

time: 214 us -> 67.9 us (0.32)
  waiting for transfers between devices: 180 us -> 0 us
  Pallas kernels: 0 us -> 61.2 us
  matrix products: 16.2 us -> 0 us
  between operations: 13.2 us -> 0.01 us
  local copies, waits for them, and re-layouts: 0.14 us -> 6.2 us
    reduce_scatter x1 -> x0, waiting for transfers between devices: 89.4 us -> none  [shards(): lax.psum_scatter(partial_value, 'tensor', scatter_dimension=1, tiled=True)]
    all_gather x4 -> x0, waiting for transfers between devices: 87.8 us -> none  [the longest x1 52.3 us: shards(): features = lax.all_gather(resid_in[0], 'tensor', axis=1, tiled=True)]
    pallas_call x0 -> x1, Pallas kernels: none -> 61.2 us  [shards(): pl.pallas_call(functools.partial(kernel, (outer, inner, dp_count)), out_s...]
    dot_general x3 -> x0, matrix products: 16.2 us -> none  [the longest x1 6.7 us: shards(): jnp.dot(arrived, parts[1], preferred_element_type=jnp.float32)]
    unnamed x4 -> x11, local copies, waits for them, and re-layouts: 0.01 us -> 6.2 us
    unnamed x5 -> x0, waiting for transfers between devices: 2.63 us -> none
  transfers between devices with their start and end apart: 6 -> 0, of which waited for: 5 -> 0; matrix products, arithmetic and copies ran while one was open for 5% -> 0% of each run, Pallas kernels for 0% -> 0%
where the time goes in v1:
time: 67.9 us; the launch traced here: 67.4 us
  Pallas kernels  61.2 us (90%)
  local copies, waits for them, and re-layouts  6.2 us (9%)
    pallas_call x1, Pallas kernels, shards(): pl.pallas_call(functools.partial(kernel, (outer, inner, dp_count)), out_s...  61.2 us
    unnamed x11, local copies, waits for them, and re-layouts  6.2 us

profile of v1, /device:TPU:4, one launch (start us, length us, event | category | flops | bytes accessed | tf_op | source)
XLA Modules:
  0.0 67.4 jit_solution(13719161210543915855)
XLA Ops:
  0.0 0.0 copy-start
  0.0 1.6 %copy-done = bf16[1,2048,512]{2,1,0:T(8,128)(2,1)S(1)} copy-done((bf16[1,2048,512]{2,1,0:T(8,128)(2,1)S(1)}, bf16[1,2048,512]{2,1,0:T(8,128)(2,1)}, u32[]{:S(2)}) %copy-start) | copy-done | bytes 2097176
  1.6 0.0 copy-start.1
  1.6 1.6 %copy-done.1 = bf16[1,512,2048]{2,1,0:T(8,128)(2,1)S(1)} copy-done((bf16[1,512,2048]{2,1,0:T(8,128)(2,1)S(1)}, bf16[1,512,2048]{2,1,0:T(8,128)(2,1)}, u32[]{:S(2)}) %copy-start.1) | copy-done | bytes 2097176
  3.2 0.0 copy-start.2
  3.2 0.9 %copy-done.2 = bf16[1,256,512]{2,1,0:T(8,128)(2,1)S(1)} copy-done((bf16[1,256,512]{2,1,0:T(8,128)(2,1)S(1)}, bf16[1,256,512]{2,1,0:T(8,128)(2,1)}, u32[]{:S(2)}) %copy-start.2) | copy-done | bytes 262168
  4.1 0.0 copy-start.3
  4.1 0.7 %copy-done.3 = f32[1,512]{1,0:T(1,128)S(1)} copy-done((f32[1,512]{1,0:T(1,128)S(1)}, f32[1,512]{1,0:T(1,128)}, u32[]{:S(2)}) %copy-start.3) | copy-done | bytes 2072
  4.8 0.0 copy-start.4
  4.8 0.7 %copy-done.4 = s32[1,2,4]{2,1,0:T(2,128)S(1)} copy-done((s32[1,2,4]{2,1,0:T(2,128)S(1)}, s32[1,2,4]{2,1,0:T(2,128)}, u32[]{:S(2)}) %copy-start.4) | copy-done | bytes 56
  5.5 61.2 %shard_map.64 = bf16[1,256,512]{2,1,0:T(8,128)(2,1)S(1)} custom-call(bf16[1,256,512]{2,1,0:T(8,128)(2,1)S(1)} %copy-done.2, f32[1,512]{1,0:T(1,128)S(1)} %copy-done.3, s32[1,2,4]{2,1,0:T(2,128)S(1)} %copy-done.4, bf16[2048,512]{1,0:T(8,128)(2,1)S(1)} %bitcast.2, bf16[512,2048]{1,0:T(8,128)(2,1)S(1)} %bitcast.3, bf16[512,2048]{1,0:T(8,128)(2,1)} %w_cross.1), custom_call_target="tpu_custom_call" | custom-call | flops 3221225472 | bytes 12582912 | tf_op jit(solution)/shard_map/pallas_call | solution.py:318
  66.7 0.7 %copy.8 = bf16[1,256,512]{2,1,0:T(8,128)(2,1)} copy(bf16[1,256,512]{2,1,0:T(8,128)(2,1)S(1)} %shard_map.64) | data formatting | bytes 524288
Async XLA Ops:
  0.0 1.6 %copy-start = (bf16[1,2048,512]{2,1,0:T(8,128)(2,1)S(1)}, bf16[1,2048,512]{2,1,0:T(8,128)(2,1)}, u32[]{:S(2)}) copy-start(bf16[1,2048,512]{2,1,0:T(8,128)(2,1)} %param.7) | copy-start | bytes 6291460
  1.6 1.6 %copy-start.1 = (bf16[1,512,2048]{2,1,0:T(8,128)(2,1)S(1)}, bf16[1,512,2048]{2,1,0:T(8,128)(2,1)}, u32[]{:S(2)}) copy-start(bf16[1,512,2048]{2,1,0:T(8,128)(2,1)} %param.10) | copy-start | bytes 6291460
  3.2 0.9 %copy-start.2 = (bf16[1,256,512]{2,1,0:T(8,128)(2,1)S(1)}, bf16[1,256,512]{2,1,0:T(8,128)(2,1)}, u32[]{:S(2)}) copy-start(bf16[1,256,512]{2,1,0:T(8,128)(2,1)} %resid.1) | copy-start | bytes 786436
  4.1 0.7 %copy-start.3 = (f32[1,512]{1,0:T(1,128)S(1)}, f32[1,512]{1,0:T(1,128)}, u32[]{:S(2)}) copy-start(f32[1,512]{1,0:T(1,128)} %thresh.1) | copy-start | bytes 6148
  4.8 0.7 %copy-start.4 = (s32[1,2,4]{2,1,0:T(2,128)S(1)}, s32[1,2,4]{2,1,0:T(2,128)}, u32[]{:S(2)}) copy-start(s32[1,2,4]{2,1,0:T(2,128)} %mask.1) | copy-start | bytes 100

commit v2 on v1

--- a/solution.py
+++ b/solution.py
@@ -12,6 +12,7 @@
 CHUNKS = 2
 GATHER_LAG = 0
 SUM_LAG = 0
+AHEAD = 3
 
 
 def grid_of(count):
@@ -27,8 +28,8 @@
 
 def kernel(
     sizes, resid, thresh, mask, w_enc, w_dec, w_cross, out,
-    feat, enc_buf, dec_buf, cross_buf, codes, early, held, own, x_out, x_in, z_out, up_in, down_in,
-    local_sem, w_send, w_recv, g_recv, g_zsend, g_xsend, c_send, c_recv, x_send, x_recv, z_send, up_recv, down_recv,
+    limits, gates, feat, enc_buf, dec_buf, cross_buf, codes, early, held, own, x_out, x_in, z_out, up_in, down_in,
+    small_sem, feat_sem, local_sem, w_send, w_recv, g_recv, g_zsend, g_xsend, c_send, c_recv, x_send, x_recv, z_send, up_recv, down_recv,
 ):
     outer, inner, dp_count = sizes
     count = outer * inner
@@ -79,8 +80,13 @@
         else:
             act()
 
-    for which in range(3):
-        when_used(which, lambda which=which: local_copy(which).start())
+    limit_copy = pltpu.make_async_copy(thresh, limits, small_sem.at[0])
+    gate_copy = pltpu.make_async_copy(mask, gates, small_sem.at[1])
+
+    def own_copy(chunk):
+        return pltpu.make_async_copy(
+            resid.at[0, pl.ds(chunk * part_rows, part_rows)], feat.at[chunk, me], feat_sem.at[chunk]
+        )
 
     barrier = pltpu.get_barrier_semaphore()
 
@@ -163,7 +169,11 @@
         for step in range(1, dp_count):
             when_used(which, lambda which=which, step=step: weight_copy(which, step).start())
     for chunk in range(CHUNKS):
-        feat[chunk, me] = resid[0, chunk * part_rows:(chunk + 1) * part_rows, :]
+        own_copy(chunk).start()
+    limit_copy.start()
+    gate_copy.start()
+    for which in range(3):
+        when_used(which, lambda which=which: local_copy(which).start())
     for chunk, distance in steps:
         if distance:
             pass_on(chunk, distance, False)
@@ -183,6 +193,7 @@
         for line in range(outer):
             for step in range(1, inner):
                 gather_arrival(chunk, line * inner + x_peer(step)).wait_recv()
+        own_copy(chunk).wait()
         total = None
         for index in range(count):
             at = (index % per_slab) * part_cols
@@ -190,10 +201,10 @@
                 feat[chunk, index], enc_buf[index // per_slab, at:at + part_cols, :], preferred_element_type=jnp.float32
             )
             total = term if total is None else total + term
-        active = jnp.maximum(total - thresh[...], 0.0)
+        active = jnp.maximum(total - limits[...], 0.0)
         tile = chunk * part_rows // TILE
         for block in range(active.shape[1] // BLOCK):
-            gate = mask[0, tile, block].astype(jnp.float32)
+            gate = gates[0, tile:tile + 1, block:block + 1].astype(jnp.float32)
             at = block * BLOCK
             codes[chunk, :, at:at + BLOCK] = (active[:, at:at + BLOCK] * gate).astype(jnp.bfloat16)
         pl.when(layer == 0)(lambda: codes_copy(chunk).start())
@@ -222,17 +233,13 @@
             device_id=to_tensor(z * inner + x_peer(step)), device_id_type=pl.DeviceIdType.MESH,
         )
 
-    def decode(chunk):
-        pl.when(layer == 1)(lambda: codes_copy(chunk).wait_recv())
-        for place in range(outer):
-            line = nth(place)
-            for step in range(1, inner):
-                share(chunk, line * inner + x_peer(step), held)
-                x_out[chunk, step - 1, line] = held[...].astype(jnp.bfloat16)
-                x_copy(chunk, step, line).start()
-        for place in range(outer):
-            line = nth(place)
-            share(chunk, line * inner + x, own.at[chunk, line])
+    def exchange(chunk, place):
+        line = nth(place)
+        for step in range(1, inner):
+            share(chunk, line * inner + x_peer(step), held)
+            x_out[chunk, step - 1, line] = held[...].astype(jnp.bfloat16)
+            x_copy(chunk, step, line).start()
+        share(chunk, line * inner + x, own.at[chunk, line])
 
     def up_copy(chunk, line):
         return pltpu.make_async_remote_copy(
@@ -279,16 +286,22 @@
             z_out[chunk, line] = total[...].astype(jnp.bfloat16)
             down_copy(chunk, line).start()
 
+    limit_copy.wait()
+    gate_copy.wait()
     weights_ready(0)
     for chunk in range(CHUNKS):
         encode(chunk)
     weights_ready(1)
     pl.when(layer == 1)(lambda: weights_ready(2))
     for chunk in range(CHUNKS):
-        decode(chunk)
+        pl.when(layer == 1)(lambda chunk=chunk: codes_copy(chunk).wait_recv())
     sums = sorted(((c, k) for c in range(CHUNKS) for k in range(outer)), key=lambda ck: (ck[1] + SUM_LAG * ck[0], ck[0]))
-    for chunk, place in sums:
-        add_up(chunk, place)
+    for at, item in enumerate(sums):
+        exchange(*item)
+        if at >= AHEAD:
+            add_up(*sums[at - AHEAD])
+    for item in sums[len(sums) - AHEAD:]:
+        add_up(*item)
 
     for chunk, distance in steps:
         pass_on(chunk, distance, True)
@@ -314,13 +327,15 @@
     bf16, f32 = jnp.bfloat16, jnp.float32
     dma = pltpu.SemaphoreType.DMA
     vmem = pl.BlockSpec(memory_space=pltpu.VMEM)
-    anywhere = pl.BlockSpec(memory_space=pl.ANY)
+    hbm = pl.BlockSpec(memory_space=pltpu.HBM)
     return pl.pallas_call(
         functools.partial(kernel, (outer, inner, dp_count)),
         out_shape=jax.ShapeDtypeStruct((1, rows, cols), bf16),
-        in_specs=[vmem, vmem, pl.BlockSpec(memory_space=pltpu.SMEM), anywhere, anywhere, anywhere],
+        in_specs=[hbm] * 6,
         out_specs=vmem,
         scratch_shapes=[
+            pltpu.VMEM((1, latents), f32),
+            pltpu.VMEM(block_mask.shape, jnp.int32),
             pltpu.VMEM((CHUNKS, count, part, cols), bf16),
             pltpu.VMEM((dp_count, deep, latents), bf16),
             pltpu.VMEM((dp_count, latents, wide), bf16),
@@ -334,6 +349,8 @@
             pltpu.VMEM((CHUNKS, outer, part, cols), bf16),
             pltpu.VMEM((CHUNKS, outer, part, cols), bf16),
             pltpu.VMEM((CHUNKS, outer, part, cols), bf16),
+            dma((2,)),
+            dma((CHUNKS,)),
             dma((3,)),
             dma((3, dp_count - 1)),
             dma((3, dp_count - 1)),
@@ -349,7 +366,7 @@
             dma((CHUNKS, outer)),
         ],
         compiler_params=pltpu.CompilerParams(
-            collective_id=0, has_side_effects=True, vmem_limit_bytes=48 * 1024 * 1024
+            collective_id=0, has_side_effects=True, vmem_limit_bytes=60 * 1024 * 1024
         ),
         cost_estimate=pl.CostEstimate(
             flops=6 * rows * latents * cols * count, bytes_accessed=6 * deep * latents * dp_count, transcendentals=0

time: 67.9 us -> 59.8 us (0.88)
  local copies, waits for them, and re-layouts: 6.2 us -> 1.67 us
  Pallas kernels: 61.2 us -> 57.2 us
    unnamed x11 -> x1, local copies, waits for them, and re-layouts: 6.2 us -> 1.67 us
    pallas_call x1, Pallas kernels: 61.2 us -> 57.2 us  [shards(): pl.pallas_call(functools.partial(kernel, (outer, inner, dp_count)), out_s...]
where the time goes in v2:
time: 59.8 us; the launch traced here: 58.9 us
  Pallas kernels  57.2 us (96%)
  local copies, waits for them, and re-layouts  1.67 us (3%)
    pallas_call x1, Pallas kernels, shards(): pl.pallas_call(functools.partial(kernel, (outer, inner, dp_count)), out_s...  57.2 us
    unnamed x1, local copies, waits for them, and re-layouts  1.67 us

profile of v2, /device:TPU:4, one launch (start us, length us, event | category | flops | bytes accessed | tf_op | source)
XLA Modules:
  0.0 58.9 jit_solution(6885615402550404153)
XLA Ops:
  0.0 57.2 %shard_map.64 = bf16[1,256,512]{2,1,0:T(8,128)(2,1)} custom-call(bf16[1,256,512]{2,1,0:T(8,128)(2,1)} %resid.1, f32[1,512]{1,0:T(1,128)} %thresh.1, s32[1,2,4]{2,1,0:T(2,128)} %mask.1, bf16[2048,512]{1,0:T(8,128)(2,1)} %bitcast.2, bf16[512,2048]{1,0:T(8,128)(2,1)} %bitcast.3, bf16[512,2048]{1,0:T(8,128)(2,1)} %w_cross.1), custom_call_target="tpu_custom_call" | custom-call | flops 3221225472 | bytes 12582912 | tf_op jit(solution)/shard_map/pallas_call | solution.py:331
  57.2 1.7 %copy.8 = bf16[1,256,512]{2,1,0:T(8,128)(2,1)} copy(bf16[1,256,512]{2,1,0:T(8,128)(2,1)} %shard_map.64) | data formatting | bytes 524288

commit v3 on v2

--- a/solution.py
+++ b/solution.py
@@ -12,7 +12,7 @@
 CHUNKS = 2
 GATHER_LAG = 0
 SUM_LAG = 0
-AHEAD = 3
+AHEAD = 4
 
 
 def grid_of(count):

time: 59.8 us -> 59 us (0.987); the launches traced: 58.9 us -> 58.9 us
  no operation moved by 1% of the time
where the time goes in v3:
time: 59 us; the launch traced here: 58.9 us
  Pallas kernels  57.2 us (97%)
  local copies, waits for them, and re-layouts  1.67 us (3%)
    pallas_call x1, Pallas kernels, shards(): pl.pallas_call(functools.partial(kernel, (outer, inner, dp_count)), out_s...  57.2 us
    unnamed x1, local copies, waits for them, and re-layouts  1.67 us

profile of v3, /device:TPU:4, one launch (start us, length us, event | category | flops | bytes accessed | tf_op | source)
XLA Modules:
  0.0 58.9 jit_solution(7701470422913401933)
XLA Ops:
  0.0 57.2 %shard_map.64 = bf16[1,256,512]{2,1,0:T(8,128)(2,1)} custom-call(bf16[1,256,512]{2,1,0:T(8,128)(2,1)} %resid.1, f32[1,512]{1,0:T(1,128)} %thresh.1, s32[1,2,4]{2,1,0:T(2,128)} %mask.1, bf16[2048,512]{1,0:T(8,128)(2,1)} %bitcast.2, bf16[512,2048]{1,0:T(8,128)(2,1)} %bitcast.3, bf16[512,2048]{1,0:T(8,128)(2,1)} %w_cross.1), custom_call_target="tpu_custom_call" | custom-call | flops 3221225472 | bytes 12582912 | tf_op jit(solution)/shard_map/pallas_call | solution.py:331
  57.2 1.7 %copy.8 = bf16[1,256,512]{2,1,0:T(8,128)(2,1)} copy(bf16[1,256,512]{2,1,0:T(8,128)(2,1)} %shard_map.64) | data formatting | bytes 524288

commit v4 on v3

--- a/solution.py
+++ b/solution.py
@@ -12,7 +12,7 @@
 CHUNKS = 2
 GATHER_LAG = 0
 SUM_LAG = 0
-AHEAD = 4
+AHEAD = 5
 
 
 def grid_of(count):

time: 59 us -> 59.9 us (1.015); the launches traced: 58.9 us -> 59 us
  no operation moved by 1% of the time
where the time goes in v4:
time: 59.9 us; the launch traced here: 59 us
  Pallas kernels  57.3 us (96%)
  local copies, waits for them, and re-layouts  1.67 us (3%)
    pallas_call x1, Pallas kernels, shards(): pl.pallas_call(functools.partial(kernel, (outer, inner, dp_count)), out_s...  57.3 us
    unnamed x1, local copies, waits for them, and re-layouts  1.67 us

profile of v4, /device:TPU:4, one launch (start us, length us, event | category | flops | bytes accessed | tf_op | source)
XLA Modules:
  0.0 59.0 jit_solution(11982586328048694247)
XLA Ops:
  0.0 57.3 %shard_map.64 = bf16[1,256,512]{2,1,0:T(8,128)(2,1)} custom-call(bf16[1,256,512]{2,1,0:T(8,128)(2,1)} %resid.1, f32[1,512]{1,0:T(1,128)} %thresh.1, s32[1,2,4]{2,1,0:T(2,128)} %mask.1, bf16[2048,512]{1,0:T(8,128)(2,1)} %bitcast.2, bf16[512,2048]{1,0:T(8,128)(2,1)} %bitcast.3, bf16[512,2048]{1,0:T(8,128)(2,1)} %w_cross.1), custom_call_target="tpu_custom_call" | custom-call | flops 3221225472 | bytes 12582912 | tf_op jit(solution)/shard_map/pallas_call | solution.py:331
  57.3 1.7 %copy.8 = bf16[1,256,512]{2,1,0:T(8,128)(2,1)} copy(bf16[1,256,512]{2,1,0:T(8,128)(2,1)} %shard_map.64) | data formatting | bytes 524288
